TPU v7x, 32 devices: a whole 2x2x4 slice. The times are simulated.
32 devices in a mesh: row: 4 (over y, x), col: 8 (over z, core).
Axes of the slice: x: 2, y: 2, z: 4, core: 2. Of those that a mesh axis runs over, the one named last changes fastest.
Arguments:
- front_orig: float32 [6144, 6144], P('row', 'col')
- pivot_shift: float32 [6144], replicated, may hold values from 4.5 to 9
- child_update: float32 [8192, 4096], P('row', 'col'), may hold values from -0.0625 to 0.0625
- child_map: int32 [2, 16], replicated, may hold values from 0 to 23, as said below
Outputs:
- front_out: float32 [6144, 6144], P('row', 'col')
Inputs may be any that keep to these rules, and one draw needn't show every extreme that they name: Child h's block b (rows and columns alike) goes to parent block child_map[h, b]; child_map[h, b] % 8 == b % 8; the two child blocks b and b + 8 (b < 8) take two different ones of the parent blocks b, b + 8, b + 16, the smaller child block to the smaller parent block.
All inputs are finite; a program needn't handle non-finite values.
Results may differ from a plain program's by a relative error of at most 0.0001.
Values sent between devices are 32-bit elements; how exact they have to be, the bound alone decides.
A program may use at most 128 MiB of HBM per device.

v0:
```python
import jax
import jax.numpy as jnp
from jax import lax
from jax.sharding import PartitionSpec as P

BS = 256
PANELS = 6


def from_partner(shard, axis, apart):
    return lax.ppermute(shard, axis, [(i, i ^ 1 << apart) for i in range(lax.axis_size(axis))])


def from_root(shard, axis, root):
    mine = lax.axis_index(axis) == root
    return lax.psum(jnp.where(mine, shard, jnp.zeros_like(shard)), axis)


def symmetric_block(pivot_block):
    return jnp.tril(pivot_block) + jnp.tril(pivot_block, -1).T


def factor_rows(pivot, panel_rows):
    factor = jnp.linalg.cholesky(symmetric_block(pivot))
    below = lax.linalg.triangular_solve(
        factor, panel_rows, left_side=False, lower=True, transpose_a=True
    )
    return (factor, below)


def on_device(front_orig, pivot_shift, child_update, child_map):
    n_row = lax.axis_size("row")
    n_col = lax.axis_size("col")
    row_id = lax.axis_index("row")
    col_id = lax.axis_index("col")
    half_rows = n_row // 2
    local_rows = front_orig.shape[0] // BS
    local_cols = front_orig.shape[1] // BS
    child_rows = child_update.shape[0] // BS
    child_cols = child_update.shape[1] // BS
    pair_count = child_rows // 2
    child_side = row_id // half_rows
    inner_row = row_id % half_rows
    holds_first = child_side == 0
    paired = child_update.reshape(pair_count, 2, BS, child_cols * BS)
    even_blocks = paired[:, 0]
    odd_blocks = paired[:, 1]
    outgoing = jnp.where(holds_first, odd_blocks, even_blocks)
    staying = jnp.where(holds_first, even_blocks, odd_blocks)
    arrived = from_partner(outgoing, "row", half_rows.bit_length() - 1)
    first_part = jnp.where(holds_first, staying, arrived)
    second_part = jnp.where(holds_first, arrived, staying)
    table_index = jnp.arange(child_map.shape[1], dtype=jnp.int32)
    row_wanted = (2 * jnp.arange(pair_count, dtype=jnp.int32) + child_side) * half_rows + inner_row
    col_wanted = jnp.arange(child_cols, dtype=jnp.int32) * n_col + col_id

    def lookup(targets, wanted):
        return jnp.sum(
            jnp.where(wanted[:, None] == table_index[None, :], targets[None, :], 0), axis=1
        )

    def place(part, child_id):
        targets = child_map[child_id]
        row_target = lookup(targets, row_wanted) // n_row
        col_target = lookup(targets, col_wanted) // n_col
        row_pick = (row_target[None, :] == jnp.arange(local_rows, dtype=jnp.int32)[:, None]).astype(
            jnp.float32
        )
        col_pick = (col_target[None, :] == jnp.arange(local_cols, dtype=jnp.int32)[:, None]).astype(
            jnp.float32
        )
        tiles = part.reshape(pair_count, BS, child_cols, BS)
        placed = jnp.einsum(
            "pq,qsjt,kj->pskt", row_pick, tiles, col_pick, precision=lax.Precision.HIGHEST
        )
        return placed.reshape(local_rows * BS, local_cols * BS)

    row_blocks = jnp.arange(local_rows, dtype=jnp.int32) * n_row + row_id
    col_blocks = jnp.arange(local_cols, dtype=jnp.int32) * n_col + col_id
    offsets = jnp.arange(BS, dtype=jnp.int32)
    row_index = (row_blocks[:, None] * BS + offsets[None, :]).reshape(-1)
    col_index = (col_blocks[:, None] * BS + offsets[None, :]).reshape(-1)
    shift_rows = lax.dynamic_index_in_dim(
        pivot_shift.reshape(local_rows, n_row, BS), row_id, axis=1, keepdims=False
    ).reshape(-1)
    diag_term = jnp.where(row_index[:, None] == col_index[None, :], shift_rows[:, None], 0.0)
    front_now = front_orig + diag_term
    front_now = front_now + place(first_part, 0)
    front_now = front_now + place(second_part, 1)
    row_of = jnp.repeat(row_blocks, BS)
    col_of = jnp.repeat(col_blocks, BS)
    stride = n_col // n_row
    pick_index = jnp.arange(local_cols, dtype=jnp.int32) * stride + col_id // n_row
    pick_table = (pick_index[:, None] == jnp.arange(local_rows, dtype=jnp.int32)[None, :]).astype(
        jnp.float32
    )
    level = row_blocks[:, None, None]
    for panel_id in range(PANELS):
        owner_row = panel_id % n_row
        owner_col = panel_id % n_col
        row_slot = panel_id // n_row
        col_slot = panel_id // n_col
        column = front_now[:, col_slot * BS : (col_slot + 1) * BS]
        pivot_local = column[row_slot * BS : (row_slot + 1) * BS]
        pivot = from_root(pivot_local, "row", owner_row)
        factor, own_rows = factor_rows(pivot, column)
        below = from_root(own_rows, "col", owner_col)
        chosen = jnp.einsum(
            "jp,pst->jst",
            pick_table,
            below.reshape(local_rows, BS, BS),
            precision=lax.Precision.HIGHEST,
        )
        across = from_root(chosen.reshape(local_cols * BS, BS), "row", col_id % n_row)
        live = (row_of > panel_id)[:, None] & (col_of > panel_id)[None, :]
        update = jnp.einsum("rk,ck->rc", below, across, precision=lax.Precision.HIGHEST)
        front_now = front_now - jnp.where(live, update, 0.0)
        tiles_now = column.reshape(local_rows, BS, BS)
        below_tiles = below.reshape(local_rows, BS, BS)
        new_column = jnp.where(
            level > panel_id, below_tiles, jnp.where(level == panel_id, factor[None], tiles_now)
        )
        new_column = new_column.reshape(local_rows * BS, BS)
        kept_column = front_now[:, col_slot * BS : (col_slot + 1) * BS]
        front_now = front_now.at[:, col_slot * BS : (col_slot + 1) * BS].set(
            jnp.where(col_id == owner_col, new_column, kept_column)
        )
    return front_now


def solution(mesh):
    in_specs = (P("row", "col"), P(), P("row", "col"), P())
    out_specs = P("row", "col")
    return jax.shard_map(
        on_device, mesh=mesh, in_specs=in_specs, out_specs=out_specs, check_vma=False
    )
```

profile of v0, /device:TPU:0, one launch (start us, length us, event | category | flops | bytes accessed | tf_op | source)
XLA Modules:
  0.0 1582.0 jit_solution(5975232951179485797)
XLA Ops:
  19.0 39.0 %collective-permute-done = f32[4,256,512]{2,1,0:T(8,128)} collective-permute-done((f32[4,256,512]{2,1,0:T(8,128)S(1)}, f32[4,256,512]{2,1,0:T(8,128)}, u32[]{:S(2)}, u32[]{:S(2)}) %collective-permute-start) | collective-permute-done | bytes 2097184 | tf_op jit(solution)/shard_map/ppermute | solution.py:11
  69.8 8.4 fusion.4
  126.3 43.8 %all-reduce.20.cloned.1.call-done = f32[256,256]{0,1:T(8,128)} async-done(((f32[256,256]{0,1:T(8,128)}), f32[256,256]{0,1:T(8,128)}) %all-reduce.20.cloned.1.call-update) | async-done | bytes 262160 | tf_op jit(solution)/shard_map/psum | solution.py:16
  172.5 11.7 cholesky.298
  184.3 9.8 custom-call.21
  194.8 11.7 cholesky.315
  213.8 19.7 %custom-call.22 = f32[2,128,128]{1,2,0:T(8,128)S(1)} custom-call(f32[2,128,128]{2,1,0:T(8,128)S(1)} %get-tuple-element.117), custom_call_target="InvertDiagBlocksLowerTriangular" | custom-call | tf_op jit(solution)/shard_map/triangular_solve/custom-call.0 | solution.py:25
  239.6 62.1 %all-reduce.22.cloned.1.call-done = f32[1536,256]{0,1:T(8,128)} async-done(((f32[1536,256]{0,1:T(8,128)}), f32[1536,256]{0,1:T(8,128)}) %all-reduce.22.cloned.1.call-update) | async-done | bytes 1572880 | tf_op jit(solution)/shard_map/psum | solution.py:16
  309.5 45.1 %all-reduce.24.cloned.1.call-done = f32[768,256]{1,0:T(8,128)} async-done(((f32[768,256]{1,0:T(8,128)}), f32[768,256]{1,0:T(8,128)}) %all-reduce.24.cloned.1.call-update) | async-done | bytes 786448 | tf_op jit(solution)/shard_map/psum | solution.py:16
  367.9 42.9 %all-reduce.26.cloned.1.call-done = f32[256,256]{0,1:T(8,128)} async-done(((f32[256,256]{0,1:T(8,128)}), f32[256,256]{0,1:T(8,128)}) %all-reduce.26.cloned.1.call-update) | async-done | bytes 262160 | tf_op jit(solution)/shard_map/psum | solution.py:16
  413.1 11.7 cholesky.332
  424.9 9.8 custom-call.23
  435.1 11.7 cholesky.349
  453.4 19.7 %custom-call.24 = f32[2,128,128]{1,2,0:T(8,128)S(1)} custom-call(f32[2,128,128]{2,1,0:T(8,128)S(1)} %get-tuple-element.118), custom_call_target="InvertDiagBlocksLowerTriangular" | custom-call | tf_op jit(solution)/shard_map/triangular_solve/custom-call.0 | solution.py:25
  477.0 62.2 %all-reduce.28.cloned.1.call-done = f32[1536,256]{0,1:T(8,128)} async-done(((f32[1536,256]{0,1:T(8,128)}), f32[1536,256]{0,1:T(8,128)}) %all-reduce.28.cloned.1.call-update) | async-done | bytes 1572880 | tf_op jit(solution)/shard_map/psum | solution.py:16
  549.0 43.1 %all-reduce.30.cloned.1.call-done = f32[768,256]{1,0:T(8,128)} async-done(((f32[768,256]{1,0:T(8,128)}), f32[768,256]{1,0:T(8,128)}) %all-reduce.30.cloned.1.call-update) | async-done | bytes 786448 | tf_op jit(solution)/shard_map/psum | solution.py:16
  607.7 42.6 %all-reduce.32.cloned.1.call-done = f32[256,256]{1,0:T(8,128)} async-done(((f32[256,256]{1,0:T(8,128)}), f32[256,256]{1,0:T(8,128)}) %all-reduce.32.cloned.1.call-update) | async-done | bytes 262160 | tf_op jit(solution)/shard_map/psum | solution.py:16
  652.7 11.7 cholesky.366
  664.4 9.8 custom-call.25
  674.7 11.7 cholesky.383
  693.4 19.7 %custom-call.26 = f32[2,128,128]{1,2,0:T(8,128)S(1)} custom-call(f32[2,128,128]{2,1,0:T(8,128)S(1)} %get-tuple-element.119), custom_call_target="InvertDiagBlocksLowerTriangular" | custom-call | tf_op jit(solution)/shard_map/triangular_solve/custom-call.0 | solution.py:25
  717.6 62.2 %all-reduce.34.cloned.1.call-done = f32[1536,256]{0,1:T(8,128)} async-done(((f32[1536,256]{0,1:T(8,128)}), f32[1536,256]{0,1:T(8,128)}) %all-reduce.34.cloned.1.call-update) | async-done | bytes 1572880 | tf_op jit(solution)/shard_map/psum | solution.py:16
  795.5 37.1 %all-reduce.36.cloned.1.call-done = f32[768,256]{1,0:T(8,128)} async-done(((f32[768,256]{1,0:T(8,128)}), f32[768,256]{1,0:T(8,128)}) %all-reduce.36.cloned.1.call-update) | async-done | bytes 786448 | tf_op jit(solution)/shard_map/psum | solution.py:16
  832.6 11.9 select_subtract_fusion.3
  850.9 42.6 %all-reduce.38.cloned.1.call-done = f32[256,256]{1,0:T(8,128)} async-done(((f32[256,256]{1,0:T(8,128)}), f32[256,256]{1,0:T(8,128)}) %all-reduce.38.cloned.1.call-update) | async-done | bytes 262160 | tf_op jit(solution)/shard_map/psum | solution.py:16
  895.9 11.7 cholesky.400
  907.7 9.8 custom-call.27
  918.0 11.7 cholesky.417
  936.5 19.7 %custom-call.28 = f32[2,128,128]{1,2,0:T(8,128)S(1)} custom-call(f32[2,128,128]{2,1,0:T(8,128)S(1)} %get-tuple-element.120), custom_call_target="InvertDiagBlocksLowerTriangular" | custom-call | tf_op jit(solution)/shard_map/triangular_solve/custom-call.0 | solution.py:25
  960.7 62.2 %all-reduce.40.cloned.1.call-done = f32[1536,256]{0,1:T(8,128)} async-done(((f32[1536,256]{0,1:T(8,128)}), f32[1536,256]{0,1:T(8,128)}) %all-reduce.40.cloned.1.call-update) | async-done | bytes 1572880 | tf_op jit(solution)/shard_map/psum | solution.py:16
  1028.2 47.6 %all-reduce.42.cloned.1.call-done = f32[768,256]{1,0:T(8,128)} async-done(((f32[768,256]{1,0:T(8,128)}), f32[768,256]{1,0:T(8,128)}) %all-reduce.42.cloned.1.call-update) | async-done | bytes 786448 | tf_op jit(solution)/shard_map/psum | solution.py:16
  1075.8 12.2 select_subtract_fusion.2
  1093.7 42.6 %all-reduce.44.cloned.1.call-done = f32[256,256]{1,0:T(8,128)} async-done(((f32[256,256]{1,0:T(8,128)}), f32[256,256]{1,0:T(8,128)}) %all-reduce.44.cloned.1.call-update) | async-done | bytes 262160 | tf_op jit(solution)/shard_map/psum | solution.py:16
  1138.7 11.7 cholesky.434
  1150.5 9.8 custom-call.29
  1160.8 11.7 cholesky.451
  1179.3 19.7 %custom-call.30 = f32[2,128,128]{1,2,0:T(8,128)S(1)} custom-call(f32[2,128,128]{2,1,0:T(8,128)S(1)} %get-tuple-element.121), custom_call_target="InvertDiagBlocksLowerTriangular" | custom-call | tf_op jit(solution)/shard_map/triangular_solve/custom-call.0 | solution.py:25
  1203.5 62.2 %all-reduce.46.cloned.1.call-done = f32[1536,256]{0,1:T(8,128)} async-done(((f32[1536,256]{0,1:T(8,128)}), f32[1536,256]{0,1:T(8,128)}) %all-reduce.46.cloned.1.call-update) | async-done | bytes 1572880 | tf_op jit(solution)/shard_map/psum | solution.py:16
  1270.9 47.6 %all-reduce.48.cloned.1.call-done = f32[768,256]{1,0:T(8,128)} async-done(((f32[768,256]{1,0:T(8,128)}), f32[768,256]{1,0:T(8,128)}) %all-reduce.48.cloned.1.call-update) | async-done | bytes 786448 | tf_op jit(solution)/shard_map/psum | solution.py:16
  1318.5 11.0 select_subtract_fusion.1
  1332.9 42.6 %all-reduce.50.cloned.1.call-done = f32[256,256]{1,0:T(8,128)} async-done(((f32[256,256]{1,0:T(8,128)}), f32[256,256]{1,0:T(8,128)}) %all-reduce.50.cloned.1.call-update) | async-done | bytes 262160 | tf_op jit(solution)/shard_map/psum | solution.py:16
  1377.9 11.7 cholesky.468
  1389.7 9.8 custom-call.31
  1400.0 11.7 cholesky.485
  1418.7 19.7 %custom-call.32 = f32[2,128,128]{1,2,0:T(8,128)S(1)} custom-call(f32[2,128,128]{2,1,0:T(8,128)S(1)} %get-tuple-element.122), custom_call_target="InvertDiagBlocksLowerTriangular" | custom-call | tf_op jit(solution)/shard_map/triangular_solve/custom-call.0 | solution.py:25
  1442.8 62.2 %all-reduce.52.cloned.1.call-done = f32[1536,256]{0,1:T(8,128)} async-done(((f32[1536,256]{0,1:T(8,128)}), f32[1536,256]{0,1:T(8,128)}) %all-reduce.52.cloned.1.call-update) | async-done | bytes 1572880 | tf_op jit(solution)/shard_map/psum | solution.py:16
  1512.3 45.5 %all-reduce.54.cloned.1.call-done = f32[768,256]{1,0:T(8,128)} async-done(((f32[768,256]{1,0:T(8,128)}), f32[768,256]{1,0:T(8,128)}) %all-reduce.54.cloned.1.call-update) | async-done | bytes 786448 | tf_op jit(solution)/shard_map/psum | solution.py:16
  1557.8 13.8 select_subtract_fusion
  (366 shorter events, 273.0 us)
Async XLA Ops:
  6.5 163.6 %all-reduce.20.cloned.1.call-start = ((), (), s32[]{:S(2)}) async-start(), calls=%async_computation | async-start | bytes 524288 | tf_op jit(solution)/shard_map/psum | solution.py:16
  6.5 5.8 copy-start.18
  9.3 48.8 %collective-permute-start = (f32[4,256,512]{2,1,0:T(8,128)S(1)}, f32[4,256,512]{2,1,0:T(8,128)}, u32[]{:S(2)}, u32[]{:S(2)}) collective-permute-start(f32[4,256,512]{2,1,0:T(8,128)S(1)} %select_bitcast_fusion), channel_id=1, source_target_pairs={{0,16},{8,24},{16,0},{24,8},{1,17},{9,25},{17,1},{25,9},{2,18},{10... | collective-permute-start | bytes 6291464 | tf_op jit(solution)/shard_map/ppermute | solution.py:11
  12.5 6.1 copy-start.19
  84.8 7.4 copy-start.11
  114.0 5.3 slice-start
  114.0 5.3 slice-start.1
  122.6 2.2 copy-start
  125.5 176.2 %all-reduce.22.cloned.1.call-start = ((), (), s32[]{:S(2)}) async-start(), calls=%async_computation.1 | async-start | bytes 3145728 | tf_op jit(solution)/shard_map/psum | solution.py:16
  239.5 115.0 %all-reduce.24.cloned.1.call-start = ((), (), s32[]{:S(2)}) async-start(), calls=%async_computation.2 | async-start | bytes 1572864 | tf_op jit(solution)/shard_map/psum | solution.py:16
  306.7 104.1 %all-reduce.26.cloned.1.call-start = ((), (), s32[]{:S(2)}) async-start(), calls=%async_computation.3 | async-start | bytes 524288 | tf_op jit(solution)/shard_map/psum | solution.py:16
  307.8 46.7 %copy-start.9 = (f32[1536,256]{0,1:T(8,128)S(1)}, f32[1536,256]{0,1:T(8,128)}, u32[]{:S(2)}) copy-start(f32[1536,256]{0,1:T(8,128)} %all-reduce.22.cloned.1.call-done) | copy-start | bytes 4718596
  354.6 8.0 copy-start.15
  367.7 171.6 %all-reduce.28.cloned.1.call-start = ((), (), s32[]{:S(2)}) async-start(), calls=%async_computation.4 | async-start | bytes 3145728 | tf_op jit(solution)/shard_map/psum | solution.py:16
  476.9 115.2 %all-reduce.30.cloned.1.call-start = ((), (), s32[]{:S(2)}) async-start(), calls=%async_computation.5 | async-start | bytes 1572864 | tf_op jit(solution)/shard_map/psum | solution.py:16
  544.2 106.1 %all-reduce.32.cloned.1.call-start = ((), (), s32[]{:S(2)}) async-start(), calls=%async_computation.6 | async-start | bytes 524288 | tf_op jit(solution)/shard_map/psum | solution.py:16
  545.8 46.3 %copy-start.10 = (f32[1536,256]{0,1:T(8,128)S(1)}, f32[1536,256]{0,1:T(8,128)}, u32[]{:S(2)}) copy-start(f32[1536,256]{0,1:T(8,128)} %all-reduce.28.cloned.1.call-done) | copy-start | bytes 4718596
  592.1 6.7 copy-start.16
  598.9 3.1 copy-start.3
  602.0 2.0 copy-start.17
  607.2 172.5 %all-reduce.34.cloned.1.call-start = ((), (), s32[]{:S(2)}) async-start(), calls=%async_computation.7 | async-start | bytes 3145728 | tf_op jit(solution)/shard_map/psum | solution.py:16
  717.5 115.0 %all-reduce.36.cloned.1.call-start = ((), (), s32[]{:S(2)}) async-start(), calls=%async_computation.8 | async-start | bytes 1572864 | tf_op jit(solution)/shard_map/psum | solution.py:16
  784.7 108.9 %all-reduce.38.cloned.1.call-start = ((), (), s32[]{:S(2)}) async-start(), calls=%async_computation.9 | async-start | bytes 524288 | tf_op jit(solution)/shard_map/psum | solution.py:16
  846.4 2.2 copy-start.2
  848.6 1.2 copy-start.6
  850.5 172.5 %all-reduce.40.cloned.1.call-start = ((), (), s32[]{:S(2)}) async-start(), calls=%async_computation.10 | async-start | bytes 3145728 | tf_op jit(solution)/shard_map/psum | solution.py:16
  895.9 60.4 %copy-start.7 = (f32[1536,256]{1,0:T(8,128)S(1)}, f32[1536,256]{1,0:T(8,128)}, u32[]{:S(2)}) copy-start(f32[1536,256]{1,0:T(8,128)} %copy-done.6) | copy-start | bytes 4718596
  960.7 115.1 %all-reduce.42.cloned.1.call-start = ((), (), s32[]{:S(2)}) async-start(), calls=%async_computation.11 | async-start | bytes 1572864 | tf_op jit(solution)/shard_map/psum | solution.py:16
  1026.8 49.0 %copy-start.12 = (f32[1536,256]{0,1:T(8,128)S(1)}, f32[1536,256]{0,1:T(8,128)}, u32[]{:S(2)}) copy-start(f32[1536,256]{0,1:T(8,128)} %all-reduce.40.cloned.1.call-done) | copy-start | bytes 4718596
  1027.8 108.5 %all-reduce.44.cloned.1.call-start = ((), (), s32[]{:S(2)}) async-start(), calls=%async_computation.12 | async-start | bytes 524288 | tf_op jit(solution)/shard_map/psum | solution.py:16
  1075.8 12.2 copy-start.8
  1092.5 107.4 %copy-start.4 = (f32[1536,256]{1,0:T(8,128)}, f32[1536,256]{1,0:T(8,128)S(1)}, u32[]{:S(2)}) copy-start(f32[1536,256]{1,0:T(8,128)S(1)} %get-tuple-element.244) | copy-start | bytes 4718596
  1093.3 172.4 %all-reduce.46.cloned.1.call-start = ((), (), s32[]{:S(2)}) async-start(), calls=%async_computation.13 | async-start | bytes 3145728 | tf_op jit(solution)/shard_map/psum | solution.py:16
  1203.5 115.0 %all-reduce.48.cloned.1.call-start = ((), (), s32[]{:S(2)}) async-start(), calls=%async_computation.14 | async-start | bytes 1572864 | tf_op jit(solution)/shard_map/psum | solution.py:16
  1269.5 49.0 %copy-start.13 = (f32[1536,256]{0,1:T(8,128)S(1)}, f32[1536,256]{0,1:T(8,128)}, u32[]{:S(2)}) copy-start(f32[1536,256]{0,1:T(8,128)} %all-reduce.46.cloned.1.call-done) | copy-start | bytes 4718596
  1270.6 105.0 %all-reduce.50.cloned.1.call-start = ((), (), s32[]{:S(2)}) async-start(), calls=%async_computation.15 | async-start | bytes 524288 | tf_op jit(solution)/shard_map/psum | solution.py:16
  1318.5 11.1 copy-start.5
  1329.5 2.2 copy-start.1
  1332.5 172.5 %all-reduce.52.cloned.1.call-start = ((), (), s32[]{:S(2)}) async-start(), calls=%async_computation.16 | async-start | bytes 3145728 | tf_op jit(solution)/shard_map/psum | solution.py:16
  1442.8 115.0 %all-reduce.54.cloned.1.call-start = ((), (), s32[]{:S(2)}) async-start(), calls=%async_computation.17 | async-start | bytes 1572864 | tf_op jit(solution)/shard_map/psum | solution.py:16
  1557.8 13.8 copy-start.14
Sparse Core Ops, SparseCore 0:
  125.7 44.4 all-reduce.19
  239.6 62.0 all-reduce.21
  306.8 47.7 all-reduce.23
  367.8 42.9 all-reduce.25
  477.1 62.1 all-reduce.27
  544.3 47.7 all-reduce.29
  607.4 42.9 all-reduce.31
  717.6 62.0 all-reduce.33
  784.8 47.7 all-reduce.35
  850.6 42.9 all-reduce.37
  960.8 62.0 all-reduce.39
  1028.0 47.7 all-reduce.41
  1093.4 42.9 all-reduce.43
  1203.6 62.0 all-reduce.45
  1270.7 47.7 all-reduce.47
  1332.6 42.9 all-reduce.49
  1442.9 62.0 all-reduce.51
  1510.0 47.6 all-reduce.53
where the time goes:
time: 1590 us; the launch traced here: 1580 us
  waiting for transfers between devices  936 us (59%)
  other arithmetic  380 us (24%)
  matrix products  120 us (8%)
  local copies, waits for them, and re-layouts  117 us (7%)
  between operations  22.6 us (1%)
    psum x18, waiting for transfers between devices, from_root(): return lax.psum(jnp.where(mine, shard, jnp.zeros_like(shard)), axis)  896 us
    another operation x42, other arithmetic, factor_rows(): factor = jnp.linalg.cholesky(symmetric_block(pivot))  208 us
    another operation x13, other arithmetic, factor_rows(): lax.linalg.triangular_solve(factor, panel_rows, left_side=False, lower=Tr...  118 us
    dot_general x6, matrix products, on_device(): jnp.einsum('rk,ck->rc', below, across, precision=lax.Precision.HIGHEST)  63.6 us
    ppermute x1, waiting for transfers between devices, from_partner(): lax.ppermute(shard, axis, [(i, i ^ 1 << apart) for i in range(lax.axis_si...  39 us
  transfers between devices with their start and end apart: 19, of which 19 were waited for; matrix products, arithmetic and copies ran while one was open for 2% of the time, Pallas kernels for 0%

commit v1 on v0

v1 whole, which is shorter than its diff:
```python
import functools

import jax
import jax.numpy as jnp
from jax import lax
from jax.experimental import pallas as pl
from jax.experimental.pallas import tpu as pltpu
from jax.sharding import PartitionSpec as P

BS = 256
PANELS = 6
STRIP = 32
VMEM_BYTES = 52 * 1024 * 1024
NT = (((1,), (1,)), ((), ()))
TN = (((0,), (0,)), ((), ()))


def split(x):
    high = x.astype(jnp.bfloat16)
    low = (x - high.astype(jnp.float32)).astype(jnp.bfloat16)
    return high, low


def mul_nt(a, b):
    a_high, a_low = a
    b_high, b_low = b
    dot = functools.partial(lax.dot_general, dimension_numbers=NT, preferred_element_type=jnp.float32)
    return dot(a_high, b_high) + (dot(a_high, b_low) + dot(a_low, b_high))


def params():
    return pltpu.CompilerParams(vmem_limit_bytes=VMEM_BYTES)


def vmem():
    return pl.BlockSpec(memory_space=pltpu.VMEM)


def smem():
    return pl.BlockSpec(memory_space=pltpu.SMEM)


def column_kernel(info_ref, front_ref, shift_ref, stay_ref, come_ref, out_ref):
    p = pl.program_id(0)
    rows = lax.broadcasted_iota(jnp.int32, (BS, BS), 0)
    cols = lax.broadcasted_iota(jnp.int32, (BS, BS), 1)
    on_diag = (rows == cols) & (info_ref[4, p] == info_ref[5, 0])
    total = front_ref[...] + jnp.where(on_diag, shift_ref[...], 0.0)
    total += jnp.where((info_ref[2, p] > 0) & (info_ref[6, 0] == 0), stay_ref[...], 0.0)
    total += jnp.where((info_ref[3, p] > 0) & (info_ref[7, 0] == 0), come_ref[0], 0.0)
    out_ref[...] = total


def panel_column(info, front, shift, child, come):
    local_rows = front.shape[0] // BS
    grid_spec = pltpu.PrefetchScalarGridSpec(
        num_scalar_prefetch=1,
        grid=(local_rows,),
        in_specs=[
            pl.BlockSpec((BS, BS), lambda p, s: (p, 0)),
            pl.BlockSpec((1, BS), lambda p, s: (0, s[4, p])),
            pl.BlockSpec((BS, BS), lambda p, s: (s[0, p], 0)),
            pl.BlockSpec((1, BS, BS), lambda p, s: (s[1, p], 0, 0)),
        ],
        out_specs=pl.BlockSpec((BS, BS), lambda p, s: (p, 0)),
    )
    return pl.pallas_call(
        column_kernel,
        grid_spec=grid_spec,
        out_shape=jax.ShapeDtypeStruct((local_rows * BS, BS), jnp.float32),
        compiler_params=params(),
    )(info, front, shift, child, come)


def cholesky_steps(work):
    row = lax.broadcasted_iota(jnp.int32, (STRIP, 1), 0)
    wide_row = lax.broadcasted_iota(jnp.int32, (STRIP, 2 * BS), 0)
    wide_col = lax.broadcasted_iota(jnp.int32, (STRIP, 2 * BS), 1)
    for strip in range(BS // STRIP):
        first = strip * STRIP
        panel = work[first : first + STRIP, :]
        for j in range(STRIP):
            column = panel[:, first + j : first + j + 1]
            factor = jnp.where(row > j, column / column[j : j + 1], 0.0)
            panel = panel - factor * panel[j : j + 1, :]
        diag = jnp.sum(jnp.where(wide_col == wide_row + first, panel, 0.0), axis=1, keepdims=True)
        scale = 1.0 / jnp.sqrt(diag)
        panel = jnp.where(wide_col >= wide_row + first, panel * scale, 0.0)
        work[first : first + STRIP, :] = panel
        after = first + STRIP
        if after < BS:
            step = lax.dot_general(
                panel[:, :BS],
                panel,
                TN,
                precision=lax.Precision.HIGHEST,
                preferred_element_type=jnp.float32,
            )
            work[after:, :] = work[after:, :] - step[after:, :]


def lead_kernel(where_block, side_ref, mine_ref, other_ref, low_ref, inv_ref, up_ref, work):
    first = side_ref[0] == 0
    for j in range(PANELS):
        for i in range(PANELS):
            dest = low_ref.at[j, i * BS : (i + 1) * BS, :]
            if i < j:
                dest[...] = jnp.zeros((BS, BS), jnp.float32)
            else:
                owner, half, place = where_block[(i, j)]
                mine = mine_ref[owner, place]
                other = other_ref[owner, place]
                dest[...] = jnp.where(first == (half == 0), mine, other)
    rows = lax.broadcasted_iota(jnp.int32, (BS, BS), 0)
    cols = lax.broadcasted_iota(jnp.int32, (BS, BS), 1)

    def step(k, carry):
        start = pl.multiple_of(k * BS, BS)
        pivot = low_ref[k, pl.ds(start, BS), :]
        work[:, :BS] = jnp.where(rows >= cols, pivot, pivot.T)
        work[:, BS:] = jnp.where(rows == cols, 1.0, 0.0)
        cholesky_steps(work)
        up_ref[k] = work[:, :BS]
        inverse = work[:, BS:]
        inv_ref[k] = inverse
        inverse = split(inverse)

        def solve(i, carry):
            at = pl.ds(pl.multiple_of(i * BS, BS), BS)
            low_ref[k, at, :] = mul_nt(split(low_ref[k, at, :]), inverse)
            return carry

        lax.fori_loop(k + 1, PANELS, solve, 0)

        def update(j, carry):
            at_j = pl.ds(pl.multiple_of(j * BS, BS), BS)
            right = split(low_ref[k, at_j, :])

            def one(i, carry):
                at = pl.ds(pl.multiple_of(i * BS, BS), BS)
                low_ref[j, at, :] = low_ref[j, at, :] - mul_nt(split(low_ref[k, at, :]), right)
                return carry

            return lax.fori_loop(j, PANELS, one, carry)

        lax.fori_loop(k + 1, PANELS, update, 0)
        return carry

    lax.fori_loop(0, PANELS, step, 0)


def factor_lead(where_block, side, mine, other):
    return pl.pallas_call(
        functools.partial(lead_kernel, where_block),
        in_specs=[smem(), vmem(), vmem()],
        out_specs=[vmem(), vmem(), vmem()],
        out_shape=[
            jax.ShapeDtypeStruct((PANELS, PANELS * BS, BS), jnp.float32),
            jax.ShapeDtypeStruct((PANELS, BS, BS), jnp.float32),
            jax.ShapeDtypeStruct((PANELS, BS, BS), jnp.float32),
        ],
        scratch_shapes=[pltpu.VMEM((BS, 2 * BS), jnp.float32)],
        compiler_params=params(),
    )(side, mine, other)


def solve_kernel(blocks, ids_ref, rows_ref, low_ref, inv_ref, out_ref):
    step = pl.program_id(0)
    done = []
    for k in range(PANELS):
        total = rows_ref[k]
        for j in range(k):
            total = total - mul_nt(done[j], split(low_ref[j, k * BS : (k + 1) * BS, :]))
        solved = mul_nt(split(total), split(inv_ref[k]))
        parts = []
        for b in range(blocks):
            live = ids_ref[step * blocks + b] > k
            parts.append(jnp.where(live, solved[b * BS : (b + 1) * BS], 0.0))
        solved = jnp.concatenate(parts, axis=0) if blocks > 1 else parts[0]
        out_ref[k] = solved
        done.append(split(solved))


def solve_rows(ids, rows, low, inv, blocks):
    count = rows.shape[1] // (blocks * BS)
    return pl.pallas_call(
        functools.partial(solve_kernel, blocks),
        grid=(count,),
        in_specs=[
            smem(),
            pl.BlockSpec((PANELS, blocks * BS, BS), lambda i: (0, i, 0)),
            vmem(),
            vmem(),
        ],
        out_specs=pl.BlockSpec((PANELS, blocks * BS, BS), lambda i: (0, i, 0)),
        out_shape=jax.ShapeDtypeStruct((PANELS, rows.shape[1], BS), jnp.float32),
        compiler_params=params(),
    )(ids, rows, low, inv)


def trail_kernel(
    head, local_cols, info_ref, front_ref, shift_ref, stay_ref, come0_ref, come1_ref,
    lead_ref, rest_ref, across_ref, factor_ref, out_ref, high_ref, low_ref,
):
    p = pl.program_id(0)

    @pl.when(p == 0)
    def _():
        for k in range(PANELS):
            high, low = split(across_ref[k])
            high_ref[k] = high
            low_ref[k] = low

    in_head = p < head
    total = jnp.zeros((BS, local_cols * BS), jnp.float32)
    for k in range(PANELS):
        left = split(jnp.where(in_head, lead_ref[k], rest_ref[k]))
        total = total + mul_nt(left, (high_ref[k], low_ref[k]))
    rows = lax.broadcasted_iota(jnp.int32, (BS, BS), 0)
    cols = lax.broadcasted_iota(jnp.int32, (BS, BS), 1)
    row_id = info_ref[4, p]
    panel = info_ref[8, 0]
    stays = info_ref[2, p] > 0
    comes = info_ref[3, p] > 0
    for s in range(local_cols):
        at = slice(s * BS, (s + 1) * BS)
        on_diag = (rows == cols) & (row_id == info_ref[5, s])
        block = front_ref[:, at] + jnp.where(on_diag, shift_ref[...], 0.0)
        for u, come_ref in enumerate((come0_ref, come1_ref)):
            piece = stay_ref[:, u * BS : (u + 1) * BS]
            block += jnp.where(stays & (info_ref[6, u] == s), piece, 0.0)
            block += jnp.where(comes & (info_ref[7, u] == s), come_ref[0], 0.0)
        block = block - total[:, at]
        if s == 0:
            own = jnp.where(in_head, lead_ref[panel], rest_ref[panel])
            in_panel = info_ref[9, 0] > 0
            block = jnp.where(in_panel & (row_id > panel), own, block)
            block = jnp.where(in_panel & (row_id == panel), factor_ref[...], block)
        out_ref[:, at] = block


def trail(info, front, shift, child, come0, come1, lead, rest, across, factor):
    local_rows = front.shape[0] // BS
    local_cols = front.shape[1] // BS
    head = lead.shape[1] // BS
    grid_spec = pltpu.PrefetchScalarGridSpec(
        num_scalar_prefetch=1,
        grid=(local_rows,),
        in_specs=[
            pl.BlockSpec((BS, local_cols * BS), lambda p, s: (p, 0)),
            pl.BlockSpec((1, BS), lambda p, s: (0, s[4, p])),
            pl.BlockSpec((BS, child.shape[1]), lambda p, s: (s[0, p], 0)),
            pl.BlockSpec((1, BS, BS), lambda p, s: (s[1, p], 0, 0)),
            pl.BlockSpec((1, BS, BS), lambda p, s: (s[1, p], 0, 0)),
            pl.BlockSpec((PANELS, BS, BS), lambda p, s: (0, jnp.minimum(p, head - 1), 0)),
            pl.BlockSpec((PANELS, BS, BS), lambda p, s: (0, jnp.maximum(p - head, 0), 0)),
            pl.BlockSpec(across.shape, lambda p, s: (0, 0, 0)),
            pl.BlockSpec((BS, BS), lambda p, s: (0, 0)),
        ],
        out_specs=pl.BlockSpec((BS, local_cols * BS), lambda p, s: (p, 0)),
        scratch_shapes=[pltpu.VMEM(across.shape, jnp.bfloat16)] * 2,
    )
    return pl.pallas_call(
        functools.partial(trail_kernel, head, local_cols),
        grid_spec=grid_spec,
        out_shape=jax.ShapeDtypeStruct(front.shape, jnp.float32),
        compiler_params=params(),
    )(info, front, shift, child, come0, come1, lead, rest, across, factor)


def on_device(front_orig, pivot_shift, child_update, child_map):
    n_row = lax.axis_size("row")
    n_col = lax.axis_size("col")
    row_id = lax.axis_index("row")
    col_id = lax.axis_index("col")
    half_rows = n_row // 2
    local_rows = front_orig.shape[0] // BS
    local_cols = front_orig.shape[1] // BS
    pair_count = child_update.shape[0] // BS // 2
    child_cols = child_update.shape[1] // BS
    stride = n_col // n_row
    head = stride
    side = row_id // half_rows

    paired = child_update.reshape(pair_count, 2, BS, child_cols, BS)
    swap = [(i, i ^ half_rows) for i in range(n_row)]
    come = [
        lax.ppermute(
            lax.dynamic_index_in_dim(paired[:, :, :, u], 1 - side, axis=1, keepdims=False),
            "row",
            swap,
        )
        for u in range(child_cols)
    ]

    mine_map = child_map[side]
    other_map = child_map[1 - side]
    slots = jnp.arange(local_rows, dtype=jnp.int32)

    def rows_of(table):
        wanted = table.reshape(pair_count, n_row)
        wanted = lax.dynamic_index_in_dim(wanted, row_id, axis=1, keepdims=False) // n_row
        hit = wanted[None, :] == slots[:, None]
        q = jnp.sum(jnp.where(hit, jnp.arange(pair_count, dtype=jnp.int32)[None, :], 0), axis=1)
        return q, jnp.any(hit, axis=1).astype(jnp.int32)

    def cols_of(table):
        wanted = table.reshape(child_cols, n_col)
        return lax.dynamic_index_in_dim(wanted, col_id, axis=1, keepdims=False) // n_col

    def line(values):
        values = jnp.atleast_1d(values).astype(jnp.int32)
        return jnp.pad(values, (0, 8 - values.shape[0]))

    stay_q, stays = rows_of(mine_map)
    come_q, comes = rows_of(other_map)
    row_blocks = slots * n_row + row_id
    col_blocks = jnp.arange(local_cols, dtype=jnp.int32) * n_col + col_id
    info = jnp.stack(
        [
            line(2 * stay_q + side),
            line(come_q),
            line(stays),
            line(comes),
            line(row_blocks),
            line(col_blocks),
            line(cols_of(mine_map)),
            line(cols_of(other_map)),
            line(jnp.minimum(col_id, PANELS - 1)),
            line(col_id < PANELS),
        ]
    )
    shift = pivot_shift.reshape(1, -1)
    column = panel_column(info, front_orig, shift, child_update, come[0])

    lead_rows = lax.all_gather(column[: head * BS], "col", axis=0)[:PANELS]
    rest_rows = lax.all_gather(column[head * BS :], "col", axis=0)[:PANELS]

    lists = [
        [(i, j) for i in range(r, PANELS, n_row) for j in range(i + 1)] for r in range(n_row)
    ]
    length = max(len(blocks) for blocks in lists)
    length += length % 2
    width = length // 2
    where_block = {}
    table = []
    for r, blocks in enumerate(lists):
        entry = [j * head + (i // n_row) for i, j in blocks]
        table.append(entry + [0] * (length - len(entry)))
        for e, block in enumerate(blocks):
            where_block[block] = (r, e // width, e % width)
    table = jnp.array(table, jnp.int32).reshape(n_row, 2, width)
    parity = col_id % 2
    picks = table[row_id, parity]
    lead_tiles = lead_rows.reshape(PANELS * head, BS, BS)
    sent = jnp.stack(
        [lax.dynamic_index_in_dim(lead_tiles, picks[e], axis=0, keepdims=False) for e in range(width)]
    )
    mine = lax.all_gather(sent, "row", axis=0)
    other = lax.ppermute(mine, "col", [(i, i ^ 1) for i in range(n_col)])
    low, inv, up = factor_lead(where_block, parity.reshape(1), mine, other)

    pick = col_id // n_row
    source = col_id % n_row
    first = lax.dynamic_index_in_dim(
        lead_rows.reshape(PANELS, 1, head, BS, BS), pick, axis=2, keepdims=False
    )
    others = lax.dynamic_index_in_dim(
        rest_rows.reshape(PANELS, local_cols - 1, head, BS, BS), pick, axis=2, keepdims=False
    )
    across = jnp.concatenate([first, others], axis=1).reshape(PANELS, local_cols * BS, BS)
    across = jnp.where(row_id == source, across, 0.0)
    bit = half_rows
    held = [0]
    while bit:
        pairs = [
            (((c % n_row) ^ h) * n_col + c, ((c % n_row) ^ h ^ bit) * n_col + c)
            for c in range(n_col)
            for h in held
        ]
        across = across + lax.ppermute(across, ("row", "col"), pairs)
        held = held + [h ^ bit for h in held]
        bit //= 2

    lead = solve_rows(row_blocks[:head], lead_rows, low, inv, head)
    rest = solve_rows(row_blocks[head:], rest_rows, low, inv, head)
    across = solve_rows(col_blocks, across, low, inv, local_cols)
    factor = lax.dynamic_index_in_dim(
        up, jnp.minimum(col_id, PANELS - 1), axis=0, keepdims=False
    ).T
    return trail(
        info, front_orig, shift, child_update, come[0], come[1], lead, rest, across, factor
    )


def solution(mesh):
    in_specs = (P("row", "col"), P(), P("row", "col"), P())
    out_specs = P("row", "col")
    return jax.shard_map(
        on_device, mesh=mesh, in_specs=in_specs, out_specs=out_specs, check_vma=False
    )
```

time: 1590 us -> 559 us (0.35)
  waiting for transfers between devices: 936 us -> 222 us
  other arithmetic: 380 us -> 11.6 us
  Pallas kernels: 0 us -> 246 us
  matrix products: 120 us -> 0 us
  local copies, waits for them, and re-layouts: 117 us -> 36 us
    psum x18 -> x0, waiting for transfers between devices: 896 us -> none  [from_root(): return lax.psum(jnp.where(mine, shard, jnp.zeros_like(shard)), axis)]
    another operation x56 -> x4, other arithmetic: 327 us -> 1.15 us  [the longest x1 1.14 us: on_device(): jnp.stack([lax.dynamic_index_in_dim(lead_tiles, picks[e], axis=0, keepdim...]
    pallas_call x0 -> x6, Pallas kernels: none -> 246 us  [the longest x1 176 us: factor_lead(): pl.pallas_call(functools.partial(lead_kernel, where_block), in_specs=[sme...]
    all_gather x0 -> x3, waiting for transfers between devices: none -> 113 us  [the longest x1 75.9 us: on_device(): rest_rows = lax.all_gather(column[head * BS:], 'col', axis=0)[:PANELS]]
    dot_general x16 -> x0, matrix products: 97.1 us -> none  [the longest x6 63.6 us: on_device(): jnp.einsum('rk,ck->rc', below, across, precision=lax.Precision.HIGHEST)]
    ppermute x1 -> x5, waiting for transfers between devices: 39 us -> 109 us  [the longest x2 83.8 us: on_device(): across = across + lax.ppermute(across, ('row', 'col'), pairs)]
    another operation x57 -> x11, local copies, waits for them, and re-layouts: 24.1 us -> 0.4 us  [the longest x2 0.16 us: rows_of(): wanted = table.reshape(pair_count, n_row)]
    another operation x30 -> x0, matrix products: 22.8 us -> none  [the longest x18 19.8 us: factor_rows(): lax.linalg.triangular_solve(factor, panel_rows, left_side=False, lower=Tr...]
  transfers between devices with their start and end apart: 19 -> 8, of which waited for: 19 -> 5; matrix products, arithmetic and copies ran while one was open for 2% -> 5% of each run, Pallas kernels for 0% -> 40%
where the time goes in v1:
time: 559 us; the launch traced here: 550 us
  Pallas kernels  246 us (44%)
  waiting for transfers between devices  222 us (40%)
  local copies, waits for them, and re-layouts  36 us (6%)
  between operations  21.2 us (4%)
  starting transfers between devices  12.9 us (2%)
  other arithmetic  11.6 us (2%)
    pallas_call x1, Pallas kernels, factor_lead(): pl.pallas_call(functools.partial(lead_kernel, where_block), in_specs=[sme...  176 us
    ppermute x2, waiting for transfers between devices, on_device(): across = across + lax.ppermute(across, ('row', 'col'), pairs)  83.8 us
    all_gather x1, waiting for transfers between devices, on_device(): rest_rows = lax.all_gather(column[head * BS:], 'col', axis=0)[:PANELS]  75.9 us
    pallas_call x3, Pallas kernels, solve_rows(): pl.pallas_call(functools.partial(solve_kernel, blocks), grid=(count,), in...  44 us
    all_gather x1, waiting for transfers between devices, on_device(): lead_rows = lax.all_gather(column[:head * BS], 'col', axis=0)[:PANELS]  37.5 us
    ppermute x2, waiting for transfers between devices, on_device(): lax.ppermute(lax.dynamic_index_in_dim(paired[:, :, :, u], 1 - side, axis=...  21.7 us
    pallas_call x1, Pallas kernels, trail(): pl.pallas_call(functools.partial(trail_kernel, head, local_cols), grid_sp...  20.2 us
  transfers between devices with their start and end apart: 8, of which 5 were waited for; matrix products, arithmetic and copies ran while one was open for 5% of the time, Pallas kernels for 40%

profile of v1, /device:TPU:0, one launch (start us, length us, event | category | flops | bytes accessed | tf_op | source)
XLA Modules:
  0.0 549.8 jit_solution(15699769441309307477)
XLA Ops:
  6.5 5.9 %reshape.96 = f32[4,2,256,2,256]{4,3,2,1,0:T(2,128)} reshape(f32[2048,512]{1,0:T(8,128)} %stay_ref.3) | data formatting | bytes 8388608 | tf_op jit(solution)/shard_map/reshape | solution.py:285
  12.4 9.1 %fusion.13 = (f32[4,2,256,1,256]{4,3,2,1,0:T(1,128)}, f32[4,2,256,1,256]{4,3,2,1,0:T(1,128)S(1)}) fusion(f32[4,2,256,2,256]{4,3,2,1,0:T(2,128)} %reshape.96), kind=kLoop, calls=%fused_computation.67 | loop fusion | bytes 8388608 | tf_op jit(solution)/shard_map/slice | solution.py:289
  21.5 0.7 constant_dynamic-slice_fusion.7
  22.3 3.0 collective-permute-start
  25.3 0.1 reshape_squeeze.13
  25.4 0.1 reshape_squeeze.12
  25.5 0.2 fusion
  25.7 0.1 fusion.2
  25.8 0.1 select_reduce_fusion
  25.9 0.1 reshape_squeeze.15
  26.0 0.1 reshape_squeeze.14
  26.1 0.2 fusion.5
  26.3 0.2 fusion.4
  26.5 0.1 select_reduce_fusion.1
  26.6 0.1 fusion.3
  26.8 21.7 %collective-permute-done.come_ref.come0_ref = f32[4,256,256]{2,1,0:T(8,128)S(1)} collective-permute-done((f32[4,256,256]{2,1,0:T(8,128)S(1)}, f32[4,256,256]{2,1,0:T(8,128)S(1)}, u32[]{:S(2)}, u32[]{:S(2)}) %collective-permute-start) | collective-permute-done | bytes 1048608 | tf_op jit(solution)/shard_map/ppermute | solution.py:288
  48.5 5.6 %shard_map.55 = f32[1536,256]{1,0:T(8,128)} custom-call(s32[10,8]{1,0:T(8,128)S(1)} %stack.62.info_ref, f32[1536,768]{1,0:T(8,128)} %front_ref.3, f32[1,6144]{1,0:T(1,128)S(1)} %bitcast.55, f32[2048,512]{1,0:T(8,128)} %stay_ref.3, f32[4,256,256]{2,1,0:T(8,128)S(1)} %collective-permute-done.come_ref.come0_ref), custom_call_target="tpu_custom_call" | custom-call | tf_op jit(solution)/shard_map/pallas_call | solution.py:67
  54.1 1.9 slice.56
  56.0 2.3 slice.58
  58.5 0.7 constant_dynamic-slice_fusion.5
  59.1 0.7 fusion.14
  67.2 37.5 %all-gather.7.cloned.1.call-done = f32[4096,256]{1,0:T(8,128)} async-done(((f32[512,256]{1,0:T(8,128)}), f32[4096,256]{1,0:T(8,128)}) %all-gather.7.cloned.1.call-update) | async-done | bytes 4194320 | tf_op jit(solution)/shard_map/all_gather | solution.py:336
  104.7 2.1 slice.57
  106.8 1.6 copy-done.2
  108.4 0.1 constant_dynamic-slice_fusion.4
  108.5 1.1 pad_maximum_fusion
  109.7 1.5 dynamic-slice_bitcast_fusion.1
  111.2 75.9 %all-gather.11.cloned.1.call-done = f32[8192,256]{1,0:T(8,128)} async-done(((f32[1024,256]{1,0:T(8,128)}), f32[8192,256]{1,0:T(8,128)}) %all-gather.11.cloned.1.call-update) | async-done | bytes 8388624 | tf_op jit(solution)/shard_map/all_gather | solution.py:337
  187.0 3.2 slice.59
  190.2 0.2 dynamic-slice_bitcast_fusion
  190.5 0.4 maximum_select_fusion
  190.9 2.1 copy-done.1
  192.9 3.8 collective-permute-start.3
  196.8 83.8 %collective-permute-done.3 = f32[6,768,256]{2,1,0:T(8,128)S(1)} collective-permute-done((f32[6,768,256]{2,1,0:T(8,128)S(1)}, f32[6,768,256]{2,1,0:T(8,128)S(1)}, u32[]{:S(2)}, u32[]{:S(2)}) %collective-permute-start.3) | collective-permute-done | bytes 4718624 | tf_op jit(solution)/shard_map/ppermute | solution.py:381
  280.6 3.1 bitcast_add_fusion
  283.7 3.5 collective-permute-start.4
  287.1 0.7 constant_dynamic-slice_fusion.6
  287.9 1.0 copy.24
  288.9 2.5 collective-permute-start.1
  291.5 3.2 collective-permute-done.2.other_ref
  294.6 176.2 %shard_map.56 = (f32[6,1536,256]{2,1,0:T(8,128)}, f32[6,256,256]{2,1,0:T(8,128)S(1)}, f32[6,256,256]{2,1,0:T(8,128)}) custom-call(s32[1]{0:T(128)} %bitcast.16.side_ref, f32[4,4,256,256]{3,2,1,0:T(8,128)} %bitcast.65, f32[4,4,256,256]{3,2,1,0:T(8,128)} %collective-permute-done.2.other_ref), custom_call_target="tpu_custom_call" | custom-call | tf_op jit(solution)/shard_map/pallas_call | solution.py:153
  470.9 1.0 constant_dynamic-slice_fusion
  471.9 0.1 copy.17
  472.0 17.3 %shard_map.58.rest_ref = f32[6,1024,256]{2,1,0:T(8,128)} custom-call(s32[4]{0:T(128)S(1)} %slice.49.ids_ref, f32[6,1024,256]{2,1,0:T(8,128)} %bitcast.59, f32[6,1536,256]{2,1,0:T(8,128)} %get-tuple-element.8.low_ref, f32[6,256,256]{2,1,0:T(8,128)S(1)} %get-tuple-element.9.inv_ref), custom_call_target="tpu_custom_call" | custom-call | tf_op jit(solution)/shard_map/pallas_call | solution.py:186
  489.3 11.7 %shard_map.57.lead_ref = f32[6,512,256]{2,1,0:T(8,128)} custom-call(s32[2]{0:T(128)S(1)} %bitcast.57, f32[6,512,256]{2,1,0:T(8,128)} %bitcast.62, f32[6,1536,256]{2,1,0:T(8,128)} %get-tuple-element.8.low_ref, f32[6,256,256]{2,1,0:T(8,128)S(1)} %get-tuple-element.9.inv_ref), custom_call_target="tpu_custom_call" | custom-call | tf_op jit(solution)/shard_map/pallas_call | solution.py:186
  501.0 6.6 %add.125.rows_ref = f32[6,768,256]{2,1,0:T(8,128)} add(f32[6,768,256]{2,1,0:T(8,128)} %bitcast_add_fusion, f32[6,768,256]{2,1,0:T(8,128)} %collective-permute-done.4) | non-fusion elementwise | flops 1179648 | bytes 14155776 | tf_op jit(solution)/shard_map/add | solution.py:381
  507.5 15.0 %shard_map.59.across_ref = f32[6,768,256]{2,1,0:T(8,128)} custom-call(s32[3]{0:T(128)S(1)} %multiply_add_fusion.ids_ref, f32[6,768,256]{2,1,0:T(8,128)} %add.125.rows_ref, f32[6,1536,256]{2,1,0:T(8,128)} %get-tuple-element.8.low_ref, f32[6,256,256]{2,1,0:T(8,128)S(1)} %get-tuple-element.9.inv_ref), custom_call_target="tpu_custom_call" | custom-call | tf_op jit(solution)/shard_map/pallas_call | solution.py:186
  522.6 20.2 %shard_map.60 = f32[1536,768]{1,0:T(8,128)} custom-call(s32[10,8]{1,0:T(8,128)S(1)} %stack.62.info_ref, f32[1536,768]{1,0:T(8,128)} %front_ref.3, f32[1,6144]{1,0:T(1,128)S(1)} %bitcast.56, f32[2048,512]{1,0:T(8,128)} %stay_ref.3, f32[4,256,256]{2,1,0:T(8,128)S(1)} %collective-permute-done.come_ref.come0_ref, ...), custom_call_target="tpu_custom_call" | custom-call | tf_op jit(solution)/shard_map/pallas_call | solution.py:263
  (37 shorter events, 0.5 us)
Async XLA Ops:
  6.5 98.1 %all-gather.7.cloned.1.call-start = ((), (), s32[]{:S(2)}) async-start(), calls=%async_computation | async-start | bytes 4718592 | tf_op jit(solution)/shard_map/all_gather | solution.py:336
  21.5 3.8 copy-start.4
  21.5 27.0 %copy-start = (f32[6144]{0:T(1024)S(1)}, f32[6144]{0:T(1024)}, u32[]{:S(2)}) copy-start(f32[6144]{0:T(1024)} %param.6) | copy-start | bytes 73732
  22.3 26.2 %collective-permute-start = (f32[4,256,256]{2,1,0:T(8,128)S(1)}, f32[4,256,256]{2,1,0:T(8,128)S(1)}, u32[]{:S(2)}, u32[]{:S(2)}) collective-permute-start(f32[4,256,256]{2,1,0:T(8,128)S(1)} %bitcast.66), channel_id=1, source_target_pairs={{0,16},{8,24},{16,0},{24,8},{1,17},{9,25},{17,1},{25,9},{2,18},{10... | collective-permute-start | bytes 3145736 | tf_op jit(solution)/shard_map/ppermute | solution.py:288
  56.0 131.1 %all-gather.11.cloned.1.call-start = ((), (), s32[]{:S(2)}) async-start(), calls=%async_computation.2 | async-start | bytes 9437184 | tf_op jit(solution)/shard_map/all_gather | solution.py:337
  58.4 228.8 %all-gather.9.cloned.1.call-start = ((), (), s32[]{:S(2)}) async-start(), calls=%async_computation.1 | async-start | bytes 5242880 | tf_op jit(solution)/shard_map/all_gather | solution.py:359
  106.8 1.6 copy-start.2
  190.2 2.7 copy-start.1
  192.9 94.2 %copy-start.3 = (f32[4,2,256,1,256]{4,3,2,1,0:T(1,128)S(1)}, f32[4,2,256,1,256]{4,3,2,1,0:T(1,128)}, u32[]{:S(2)}) copy-start(f32[4,2,256,1,256]{4,3,2,1,0:T(1,128)} %get-tuple-element.13) | copy-start | bytes 6291460
  192.9 87.6 %collective-permute-start.3 = (f32[6,768,256]{2,1,0:T(8,128)S(1)}, f32[6,768,256]{2,1,0:T(8,128)S(1)}, u32[]{:S(2)}, u32[]{:S(2)}) collective-permute-start(f32[6,768,256]{2,1,0:T(8,128)S(1)} %bitcast.63), channel_id=1, source_target_pairs={{0,16},{9,25},{18,2},{27,11},{4,20},{13,29},{22,6},{31,15}} | collective-permute-start | bytes 14155784 | tf_op jit(solution)/shard_map/ppermute | solution.py:381
  283.7 217.3 %collective-permute-start.4 = (f32[6,768,256]{2,1,0:T(8,128)}, f32[6,768,256]{2,1,0:T(8,128)}, u32[]{:S(2)}, u32[]{:S(2)}) collective-permute-start(f32[6,768,256]{2,1,0:T(8,128)} %bitcast_add_fusion), channel_id=1, source_target_pairs={{0,8},{16,24},{9,1},{25,17},{18,26},{2,10},{27,19},{11,3},{4,12},{... | collective-permute-start | bytes 14155784 | tf_op jit(solution)/shard_map/ppermute | solution.py:381
  287.1 7.5 %collective-permute-start.2 = (f32[4,4,256,256]{3,2,1,0:T(8,128)}, f32[4,4,256,256]{3,2,1,0:T(8,128)}, u32[]{:S(2)}, u32[]{:S(2)}) collective-permute-start(f32[4,4,256,256]{3,2,1,0:T(8,128)} %bitcast.64), channel_id=1, source_target_pairs={{0,1},{1,0},{2,3},{3,2},{4,5},{5,4},{6,7},{7,6},{8,9},{9,8},{10,11... | collective-permute-start | bytes 12582920 | tf_op jit(solution)/shard_map/ppermute | solution.py:360
  288.9 233.7 %collective-permute-start.1 = (f32[4,256,256]{2,1,0:T(8,128)}, f32[4,256,256]{2,1,0:T(8,128)}, u32[]{:S(2)}, u32[]{:S(2)}) collective-permute-start(f32[4,256,256]{2,1,0:T(8,128)} %bitcast.51), channel_id=1, source_target_pairs={{0,16},{8,24},{16,0},{24,8},{1,17},{9,25},{17,1},{25,9},{2,18},{10... | collective-permute-start | bytes 3145736 | tf_op jit(solution)/shard_map/ppermute | solution.py:288
Sparse Core Ops, SparseCore 0:
  56.1 48.5 all-gather.6
  106.3 80.7 all-gather.10
  188.9 65.8 all-gather.8

commit v2 on v1

--- a/solution.py
+++ b/solution.py
@@ -10,6 +10,7 @@
 BS = 256
 PANELS = 6
 STRIP = 32
+GROUP = 2
 VMEM_BYTES = 52 * 1024 * 1024
 NT = (((1,), (1,)), ((), ()))
 TN = (((0,), (0,)), ((), ()))
@@ -74,29 +75,33 @@
 
 def cholesky_steps(work):
     row = lax.broadcasted_iota(jnp.int32, (STRIP, 1), 0)
-    wide_row = lax.broadcasted_iota(jnp.int32, (STRIP, 2 * BS), 0)
-    wide_col = lax.broadcasted_iota(jnp.int32, (STRIP, 2 * BS), 1)
+    half = BS // 2
     for strip in range(BS // STRIP):
         first = strip * STRIP
-        panel = work[first : first + STRIP, :]
+        after = first + STRIP
+        lo = first // half * half
+        hi = BS + (after + half - 1) // half * half
+        wide_row = lax.broadcasted_iota(jnp.int32, (STRIP, hi - lo), 0) + first
+        wide_col = lax.broadcasted_iota(jnp.int32, (STRIP, hi - lo), 1) + lo
+        panel = work[first:after, lo:hi]
         for j in range(STRIP):
-            column = panel[:, first + j : first + j + 1]
+            at = first - lo + j
+            column = panel[:, at : at + 1]
             factor = jnp.where(row > j, column / column[j : j + 1], 0.0)
             panel = panel - factor * panel[j : j + 1, :]
-        diag = jnp.sum(jnp.where(wide_col == wide_row + first, panel, 0.0), axis=1, keepdims=True)
+        diag = jnp.sum(jnp.where(wide_col == wide_row, panel, 0.0), axis=1, keepdims=True)
         scale = 1.0 / jnp.sqrt(diag)
-        panel = jnp.where(wide_col >= wide_row + first, panel * scale, 0.0)
-        work[first : first + STRIP, :] = panel
-        after = first + STRIP
+        panel = jnp.where(wide_col >= wide_row, panel * scale, 0.0)
+        work[first:after, lo:hi] = panel
         if after < BS:
             step = lax.dot_general(
-                panel[:, :BS],
+                panel[:, : BS - lo],
                 panel,
                 TN,
                 precision=lax.Precision.HIGHEST,
                 preferred_element_type=jnp.float32,
             )
-            work[after:, :] = work[after:, :] - step[after:, :]
+            work[after:, lo:hi] = work[after:, lo:hi] - step[after - lo :, :]
 
 
 def lead_kernel(where_block, side_ref, mine_ref, other_ref, low_ref, inv_ref, up_ref, work):
@@ -111,6 +116,15 @@
                 mine = mine_ref[owner, place]
                 other = other_ref[owner, place]
                 dest[...] = jnp.where(first == (half == 0), mine, other)
+    factor_panels(0, low_ref, inv_ref, up_ref, work)
+
+
+def more_kernel(start, before_ref, low_ref, inv_ref, up_ref, work):
+    low_ref[...] = before_ref[...]
+    factor_panels(start, low_ref, inv_ref, up_ref, work)
+
+
+def factor_panels(begin, low_ref, inv_ref, up_ref, work):
     rows = lax.broadcasted_iota(jnp.int32, (BS, BS), 0)
     cols = lax.broadcasted_iota(jnp.int32, (BS, BS), 1)
 
@@ -120,9 +134,9 @@
         work[:, :BS] = jnp.where(rows >= cols, pivot, pivot.T)
         work[:, BS:] = jnp.where(rows == cols, 1.0, 0.0)
         cholesky_steps(work)
-        up_ref[k] = work[:, :BS]
+        up_ref[k - begin] = jnp.where(cols >= rows, work[:, :BS], 0.0)
         inverse = work[:, BS:]
-        inv_ref[k] = inverse
+        inv_ref[k - begin] = inverse
         inverse = split(inverse)
 
         def solve(i, carry):
@@ -146,22 +160,25 @@
         lax.fori_loop(k + 1, PANELS, update, 0)
         return carry
 
-    lax.fori_loop(0, PANELS, step, 0)
-
-
-def factor_lead(where_block, side, mine, other):
+    lax.fori_loop(begin, begin + GROUP, step, 0)
+
+
+def factor_group(kernel, operands, in_specs):
     return pl.pallas_call(
-        functools.partial(lead_kernel, where_block),
-        in_specs=[smem(), vmem(), vmem()],
+        kernel,
+        in_specs=in_specs,
         out_specs=[vmem(), vmem(), vmem()],
         out_shape=[
             jax.ShapeDtypeStruct((PANELS, PANELS * BS, BS), jnp.float32),
-            jax.ShapeDtypeStruct((PANELS, BS, BS), jnp.float32),
-            jax.ShapeDtypeStruct((PANELS, BS, BS), jnp.float32),
+            jax.ShapeDtypeStruct((GROUP, BS, BS), jnp.float32),
+            jax.ShapeDtypeStruct((GROUP, BS, BS), jnp.float32),
         ],
         scratch_shapes=[pltpu.VMEM((BS, 2 * BS), jnp.float32)],
+        cost_estimate=pl.CostEstimate(
+            flops=60_000_000_000, bytes_accessed=200_000_000, transcendentals=0
+        ),
         compiler_params=params(),
-    )(side, mine, other)
+    )(*operands)
 
 
 def solve_kernel(blocks, ids_ref, rows_ref, low_ref, inv_ref, out_ref):
@@ -334,7 +351,6 @@
     column = panel_column(info, front_orig, shift, child_update, come[0])
 
     lead_rows = lax.all_gather(column[: head * BS], "col", axis=0)[:PANELS]
-    rest_rows = lax.all_gather(column[head * BS :], "col", axis=0)[:PANELS]
 
     lists = [
         [(i, j) for i in range(r, PANELS, n_row) for j in range(i + 1)] for r in range(n_row)
@@ -358,7 +374,15 @@
     )
     mine = lax.all_gather(sent, "row", axis=0)
     other = lax.ppermute(mine, "col", [(i, i ^ 1) for i in range(n_col)])
-    low, inv, up = factor_lead(where_block, parity.reshape(1), mine, other)
+
+    other, rest_part = lax.optimization_barrier((other, column[head * BS :]))
+    rest_rows = lax.all_gather(rest_part, "col", axis=0)[:PANELS]
+    low, inv, up = factor_group(
+        functools.partial(lead_kernel, where_block),
+        (parity.reshape(1), mine, other),
+        [smem(), vmem(), vmem()],
+    )
+    inverses, factors = [inv], [up]
 
     pick = col_id // n_row
     source = col_id % n_row
@@ -370,17 +394,28 @@
     )
     across = jnp.concatenate([first, others], axis=1).reshape(PANELS, local_cols * BS, BS)
     across = jnp.where(row_id == source, across, 0.0)
+    across, low = lax.optimization_barrier((across, low))
     bit = half_rows
     held = [0]
+    begin = GROUP
     while bit:
         pairs = [
             (((c % n_row) ^ h) * n_col + c, ((c % n_row) ^ h ^ bit) * n_col + c)
             for c in range(n_col)
             for h in held
         ]
-        across = across + lax.ppermute(across, ("row", "col"), pairs)
+        came = lax.ppermute(across, ("row", "col"), pairs)
+        if begin < PANELS:
+            low, inv, up = factor_group(functools.partial(more_kernel, begin), (low,), [vmem()])
+            inverses.append(inv)
+            factors.append(up)
+            begin += GROUP
+            came, low = lax.optimization_barrier((came, low))
+        across = across + came
         held = held + [h ^ bit for h in held]
         bit //= 2
+    inv = jnp.concatenate(inverses, axis=0)
+    up = jnp.concatenate(factors, axis=0)
 
     lead = solve_rows(row_blocks[:head], lead_rows, low, inv, head)
     rest = solve_rows(row_blocks[head:], rest_rows, low, inv, head)

time: 559 us -> 474 us (0.85)
  waiting for transfers between devices: 222 us -> 125 us
  Pallas kernels: 246 us -> 257 us
    ppermute x2, waiting for transfers between devices: 83.8 us -> 0.01 us  [on_device(): came = lax.ppermute(across, ('row', 'col'), pairs)]
    all_gather x1, waiting for transfers between devices: 75.9 us -> 7.72 us  [on_device(): rest_rows = lax.all_gather(rest_part, 'col', axis=0)[:PANELS]]
    all_gather x1, waiting for transfers between devices: 0.01 us -> 51.3 us  [on_device(): mine = lax.all_gather(sent, 'row', axis=0)]
    pallas_call x1 -> x3, Pallas kernels: 176 us -> 188 us  [factor_group(): pl.pallas_call(kernel, in_specs=in_specs, out_specs=[vmem(), vmem(), vmem...]
  transfers between devices with their start and end apart: 8 -> 8, of which waited for: 5 -> 5; matrix products, arithmetic and copies ran while one was open for 5% -> 5% of each run, Pallas kernels for 40% -> 50%
where the time goes in v2:
time: 474 us; the launch traced here: 468 us
  Pallas kernels  257 us (54%)
  waiting for transfers between devices  125 us (26%)
  local copies, waits for them, and re-layouts  34.8 us (7%)
  between operations  21.3 us (4%)
  starting transfers between devices  14.6 us (3%)
  other arithmetic  14.1 us (3%)
    pallas_call x3, Pallas kernels, factor_group(): pl.pallas_call(kernel, in_specs=in_specs, out_specs=[vmem(), vmem(), vmem...  188 us
    all_gather x1, waiting for transfers between devices, on_device(): mine = lax.all_gather(sent, 'row', axis=0)  51.3 us
    pallas_call x3, Pallas kernels, solve_rows(): pl.pallas_call(functools.partial(solve_kernel, blocks), grid=(count,), in...  44 us
    all_gather x1, waiting for transfers between devices, on_device(): lead_rows = lax.all_gather(column[:head * BS], 'col', axis=0)[:PANELS]  39.5 us
    ppermute x2, waiting for transfers between devices, on_device(): lax.ppermute(lax.dynamic_index_in_dim(paired[:, :, :, u], 1 - side, axis=...  21.6 us
    pallas_call x1, Pallas kernels, trail(): pl.pallas_call(functools.partial(trail_kernel, head, local_cols), grid_sp...  20 us
    add x2, other arithmetic, on_device(): across = across + came  12 us
    ppermute x2, starting transfers between devices, on_device(): came = lax.ppermute(across, ('row', 'col'), pairs)  9.79 us
  transfers between devices with their start and end apart: 8, of which 5 were waited for; matrix products, arithmetic and copies ran while one was open for 5% of the time, Pallas kernels for 50%

profile of v2, /device:TPU:0, one launch (start us, length us, event | category | flops | bytes accessed | tf_op | source)
XLA Modules:
  0.0 467.7 jit_solution(1196943499893967751)
XLA Ops:
  6.5 5.9 %reshape.96 = f32[4,2,256,2,256]{4,3,2,1,0:T(2,128)} reshape(f32[2048,512]{1,0:T(8,128)} %stay_ref.3) | data formatting | bytes 8388608 | tf_op jit(solution)/shard_map/reshape | solution.py:302
  12.4 9.0 %fusion.15 = (f32[4,2,256,1,256]{4,3,2,1,0:T(1,128)}, f32[4,2,256,1,256]{4,3,2,1,0:T(1,128)S(1)}) fusion(f32[4,2,256,2,256]{4,3,2,1,0:T(2,128)} %reshape.96), kind=kLoop, calls=%fused_computation.73 | loop fusion | bytes 8388608 | tf_op jit(solution)/shard_map/slice | solution.py:306
  21.4 0.7 constant_dynamic-slice_fusion.6
  22.2 3.0 collective-permute-start
  25.2 0.1 reshape_squeeze.12
  25.3 0.1 reshape_squeeze.13
  25.4 0.2 fusion.2
  25.6 0.1 select_reduce_fusion.1
  25.7 0.1 fusion.5
  25.8 0.1 select_reduce_fusion
  26.0 0.1 reshape_squeeze.15
  26.1 0.2 fusion.7
  26.3 0.2 fusion.6
  26.5 0.1 fusion.4
  26.7 21.6 %collective-permute-done.come_ref.come0_ref = f32[4,256,256]{2,1,0:T(8,128)S(1)} collective-permute-done((f32[4,256,256]{2,1,0:T(8,128)S(1)}, f32[4,256,256]{2,1,0:T(8,128)S(1)}, u32[]{:S(2)}, u32[]{:S(2)}) %collective-permute-start) | collective-permute-done | bytes 1048608 | tf_op jit(solution)/shard_map/ppermute | solution.py:305
  48.3 5.6 %shard_map.55 = f32[1536,256]{1,0:T(8,128)} custom-call(s32[10,8]{1,0:T(8,128)S(1)} %stack.62.info_ref, f32[1536,768]{1,0:T(8,128)} %front_ref.3, f32[1,6144]{1,0:T(1,128)S(1)} %bitcast.54, f32[2048,512]{1,0:T(8,128)} %stay_ref.3, f32[4,256,256]{2,1,0:T(8,128)S(1)} %collective-permute-done.come_ref.come0_ref), custom_call_target="tpu_custom_call" | custom-call | tf_op jit(solution)/shard_map/pallas_call | solution.py:68
  54.0 1.9 slice.56
  56.0 0.7 constant_dynamic-slice_fusion.4
  56.6 0.7 fusion.16
  65.0 39.5 %all-gather.7.cloned.1.call-done = f32[4096,256]{1,0:T(8,128)} async-done(((f32[512,256]{1,0:T(8,128)}), f32[4096,256]{1,0:T(8,128)}) %all-gather.7.cloned.1.call-update) | async-done | bytes 4194320 | tf_op jit(solution)/shard_map/all_gather | solution.py:353
  104.5 2.1 slice.57
  106.7 0.1 constant_dynamic-slice_fusion.3
  106.8 1.2 pad_maximum_fusion
  108.0 0.3 all-gather.11.cloned.1.call-start
  108.3 51.3 %all-gather.9.cloned.1.call-done = f32[16,256,256]{2,1,0:T(8,128)} async-done(((f32[4,256,256]{2,1,0:T(8,128)}), f32[16,256,256]{2,1,0:T(8,128)}) %all-gather.9.cloned.1.call-update) | async-done | bytes 4194320 | tf_op jit(solution)/shard_map/all_gather | solution.py:375
  159.6 2.3 slice.58
  161.9 5.2 %collective-permute-done.2.other_ref = f32[4,4,256,256]{3,2,1,0:T(8,128)} collective-permute-done((f32[4,4,256,256]{3,2,1,0:T(8,128)}, f32[4,4,256,256]{3,2,1,0:T(8,128)}, u32[]{:S(2)}, u32[]{:S(2)}) %collective-permute-start.2) | collective-permute-done | bytes 4194336 | tf_op jit(solution)/shard_map/ppermute | solution.py:376
  167.1 2.0 constant_dynamic-slice_fusion.5
  169.1 1.0 copy.24
  170.1 1.5 collective-permute-start.1
  171.7 1.2 dynamic-slice_bitcast_fusion.1
  172.9 68.7 %shard_map.56 = (f32[6,1536,256]{2,1,0:T(8,128)}, f32[2,256,256]{2,1,0:T(8,128)S(1)}, f32[2,256,256]{2,1,0:T(8,128)S(1)}) custom-call(s32[1]{0:T(128)} %bitcast.27.side_ref, f32[4,4,256,256]{3,2,1,0:T(8,128)} %bitcast.66, f32[4,4,256,256]{3,2,1,0:T(8,128)} %collective-permute-done.2.other_ref), custom_call_target="tpu_custom_call" | custom-call | flops 60000002048 | bytes 200000000 | tf_op jit(solution)/shard_map/pallas_call | solution.py:167
  241.6 7.7 %all-gather.11.cloned.1.call-done = f32[8192,256]{1,0:T(8,128)} async-done(((f32[1024,256]{1,0:T(8,128)}), f32[8192,256]{1,0:T(8,128)}) %all-gather.11.cloned.1.call-update) | async-done | bytes 8388624 | tf_op jit(solution)/shard_map/all_gather | solution.py:379
  249.3 3.2 slice.59
  252.6 0.2 dynamic-slice_bitcast_fusion
  252.8 2.4 copy-done.10
  255.2 0.4 maximum_select_fusion
  255.6 5.9 %collective-permute-start.3 = (f32[6,768,256]{2,1,0:T(8,128)S(1)}, f32[6,768,256]{2,1,0:T(8,128)}, u32[]{:S(2)}, u32[]{:S(2)}) collective-permute-start(f32[6,768,256]{2,1,0:T(8,128)S(1)} %bitcast.62), channel_id=1, source_target_pairs={{0,16},{9,25},{18,2},{27,11},{4,20},{13,29},{22,6},{31,15}} | collective-permute-start | bytes 14155784 | tf_op jit(solution)/shard_map/ppermute | solution.py:407
  261.5 61.5 %shard_map.57 = (f32[6,1536,256]{2,1,0:T(8,128)}, f32[2,256,256]{2,1,0:T(8,128)S(1)}, f32[2,256,256]{2,1,0:T(8,128)S(1)}) custom-call(f32[6,1536,256]{2,1,0:T(8,128)} %get-tuple-element.26.before_ref), custom_call_target="tpu_custom_call" | custom-call | flops 60000002048 | bytes 200000000 | tf_op jit(solution)/shard_map/pallas_call | solution.py:167
  323.0 5.4 %add.124 = f32[6,768,256]{2,1,0:T(8,128)} add(f32[6,768,256]{2,1,0:T(8,128)S(1)} %bitcast.63, f32[6,768,256]{2,1,0:T(8,128)} %collective-permute-done.3) | non-fusion elementwise | flops 1179648 | bytes 14155776 | tf_op jit(solution)/shard_map/add | solution.py:414
  328.5 3.9 collective-permute-start.4
  332.4 57.6 %shard_map.58 = (f32[6,1536,256]{2,1,0:T(8,128)}, f32[2,256,256]{2,1,0:T(8,128)S(1)}, f32[2,256,256]{2,1,0:T(8,128)S(1)}) custom-call(f32[6,1536,256]{2,1,0:T(8,128)} %get-tuple-element.29.before_ref), custom_call_target="tpu_custom_call" | custom-call | flops 60000002048 | bytes 200000000 | tf_op jit(solution)/shard_map/pallas_call | solution.py:167
  390.1 0.1 copy.17
  390.3 6.6 %add.125.rows_ref = f32[6,768,256]{2,1,0:T(8,128)} add(f32[6,768,256]{2,1,0:T(8,128)} %add.124, f32[6,768,256]{2,1,0:T(8,128)} %collective-permute-done.4) | non-fusion elementwise | flops 1179648 | bytes 14155776 | tf_op jit(solution)/shard_map/add | solution.py:414
  396.9 15.0 %shard_map.61.across_ref = f32[6,768,256]{2,1,0:T(8,128)} custom-call(s32[3]{0:T(128)S(1)} %copy-done.7, f32[6,768,256]{2,1,0:T(8,128)} %add.125.rows_ref, f32[6,1536,256]{2,1,0:T(8,128)} %get-tuple-element.31.low_ref, f32[6,256,256]{2,1,0:T(8,128)S(1)} %constant_dynamic-update-slice_fusion.inv_ref), custom_call_target="tpu_custom_call" | custom-call | tf_op jit(solution)/shard_map/pallas_call | solution.py:203
  411.9 11.7 %shard_map.59.lead_ref = f32[6,512,256]{2,1,0:T(8,128)} custom-call(s32[2]{0:T(128)S(1)} %bitcast.56, f32[6,512,256]{2,1,0:T(8,128)} %bitcast.61, f32[6,1536,256]{2,1,0:T(8,128)} %get-tuple-element.31.low_ref, f32[6,256,256]{2,1,0:T(8,128)S(1)} %constant_dynamic-update-slice_fusion.inv_ref), custom_call_target="tpu_custom_call" | custom-call | tf_op jit(solution)/shard_map/pallas_call | solution.py:203
  423.5 17.4 %shard_map.60.rest_ref = f32[6,1024,256]{2,1,0:T(8,128)} custom-call(s32[4]{0:T(128)S(1)} %slice.51.ids_ref, f32[6,1024,256]{2,1,0:T(8,128)} %bitcast.58, f32[6,1536,256]{2,1,0:T(8,128)} %get-tuple-element.31.low_ref, f32[6,256,256]{2,1,0:T(8,128)S(1)} %constant_dynamic-update-slice_fusion.inv_ref), custom_call_target="tpu_custom_call" | custom-call | tf_op jit(solution)/shard_map/pallas_call | solution.py:203
  440.9 20.0 %shard_map.62 = f32[1536,768]{1,0:T(8,128)} custom-call(s32[10,8]{1,0:T(8,128)S(1)} %copy-done.5, f32[1536,768]{1,0:T(8,128)} %front_ref.3, f32[1,6144]{1,0:T(1,128)S(1)} %bitcast.55, f32[2048,512]{1,0:T(8,128)} %stay_ref.3, f32[4,256,256]{2,1,0:T(8,128)S(1)} %copy-done.1, f32[4,256,256]{2,1,0:T(8,128)} %collective-permute-done.1.come1_ref, ...), custom_call_target="tpu_custom_call" | custom-call | tf_op jit(solution)/shard_map/pallas_call | solution.py:280
  (60 shorter events, 0.7 us)
Async XLA Ops:
  6.5 98.0 %all-gather.7.cloned.1.call-start = ((), (), s32[]{:S(2)}) async-start(), calls=%async_computation | async-start | bytes 4718592 | tf_op jit(solution)/shard_map/all_gather | solution.py:353
  21.3 3.8 copy-start.13
  21.3 27.0 %copy-start.2 = (f32[6144]{0:T(1024)S(1)}, f32[6144]{0:T(1024)}, u32[]{:S(2)}) copy-start(f32[6144]{0:T(1024)} %param.6) | copy-start | bytes 73732
  22.2 26.2 %collective-permute-start = (f32[4,256,256]{2,1,0:T(8,128)S(1)}, f32[4,256,256]{2,1,0:T(8,128)S(1)}, u32[]{:S(2)}, u32[]{:S(2)}) collective-permute-start(f32[4,256,256]{2,1,0:T(8,128)S(1)} %bitcast.64), channel_id=1, source_target_pairs={{0,16},{8,24},{16,0},{24,8},{1,17},{9,25},{17,1},{25,9},{2,18},{10... | collective-permute-start | bytes 3145736 | tf_op jit(solution)/shard_map/ppermute | solution.py:305
  25.8 145.8 %copy-start.8 = (s32[6]{0:T(128)}, s32[6]{0:T(128)S(1)}, u32[]{:S(2)}) copy-start(s32[6]{0:T(128)S(1)} %multiply_add_fusion.1) | copy-start | bytes 76
  25.9 0.7 copy-start.6
  26.7 27.3 %copy-start.4 = (s32[10,8]{1,0:T(8,128)}, s32[10,8]{1,0:T(8,128)S(1)}, u32[]{:S(2)}) copy-start(s32[10,8]{1,0:T(8,128)S(1)} %stack.62.info_ref) | copy-start | bytes 964
  48.3 5.7 %copy-start = (f32[4,256,256]{2,1,0:T(8,128)}, f32[4,256,256]{2,1,0:T(8,128)S(1)}, u32[]{:S(2)}) copy-start(f32[4,256,256]{2,1,0:T(8,128)S(1)} %collective-permute-done.come_ref.come0_ref) | copy-start | bytes 3145732
  55.9 103.7 %all-gather.9.cloned.1.call-start = ((), (), s32[]{:S(2)}) async-start(), calls=%async_computation.1 | async-start | bytes 5242880 | tf_op jit(solution)/shard_map/all_gather | solution.py:375
  106.6 65.0 %copy-start.11 = (f32[3072,256]{1,0:T(8,128)}, f32[3072,256]{1,0:T(8,128)S(1)}, u32[]{:S(2)}) copy-start(f32[3072,256]{1,0:T(8,128)S(1)} %slice.57) | copy-start | bytes 9437188
  108.0 141.3 %all-gather.11.cloned.1.call-start = ((), (), s32[]{:S(2)}) async-start(), calls=%async_computation.2 | async-start | bytes 9437184 | tf_op jit(solution)/shard_map/all_gather | solution.py:379
  159.6 7.5 %collective-permute-start.2 = (f32[4,4,256,256]{3,2,1,0:T(8,128)}, f32[4,4,256,256]{3,2,1,0:T(8,128)}, u32[]{:S(2)}, u32[]{:S(2)}) collective-permute-start(f32[4,4,256,256]{3,2,1,0:T(8,128)} %bitcast.65), channel_id=1, source_target_pairs={{0,1},{1,0},{2,3},{3,2},{4,5},{5,4},{6,7},{7,6},{8,9},{9,8},{10,11... | collective-permute-start | bytes 12582920 | tf_op jit(solution)/shard_map/ppermute | solution.py:376
  170.1 270.8 %collective-permute-start.1 = (f32[4,256,256]{2,1,0:T(8,128)}, f32[4,256,256]{2,1,0:T(8,128)}, u32[]{:S(2)}, u32[]{:S(2)}) collective-permute-start(f32[4,256,256]{2,1,0:T(8,128)} %bitcast.50), channel_id=1, source_target_pairs={{0,16},{8,24},{16,0},{24,8},{1,17},{9,25},{17,1},{25,9},{2,18},{10... | collective-permute-start | bytes 3145736 | tf_op jit(solution)/shard_map/ppermute | solution.py:305
  252.5 2.7 copy-start.10
  252.5 2.7 copy-start.12
  255.6 67.5 %collective-permute-start.3 = (f32[6,768,256]{2,1,0:T(8,128)S(1)}, f32[6,768,256]{2,1,0:T(8,128)}, u32[]{:S(2)}, u32[]{:S(2)}) collective-permute-start(f32[6,768,256]{2,1,0:T(8,128)S(1)} %bitcast.62), channel_id=1, source_target_pairs={{0,16},{9,25},{18,2},{27,11},{4,20},{13,29},{22,6},{31,15}} | collective-permute-start | bytes 14155784 | tf_op jit(solution)/shard_map/ppermute | solution.py:407
  328.5 61.8 %collective-permute-start.4 = (f32[6,768,256]{2,1,0:T(8,128)}, f32[6,768,256]{2,1,0:T(8,128)}, u32[]{:S(2)}, u32[]{:S(2)}) collective-permute-start(f32[6,768,256]{2,1,0:T(8,128)} %add.124), channel_id=1, source_target_pairs={{0,8},{16,24},{9,1},{25,17},{18,26},{2,10},{27,19},{11,3},{4,12},{... | collective-permute-start | bytes 14155784 | tf_op jit(solution)/shard_map/ppermute | solution.py:407
  390.3 6.6 %copy-start.7 = (s32[3]{0:T(128)S(1)}, s32[3]{0:T(128)}, u32[]{:S(2)}) copy-start(s32[3]{0:T(128)} %copy-done.6) | copy-start | bytes 40
  396.9 15.0 %copy-start.9 = (s32[6]{0:T(128)S(1)}, s32[6]{0:T(128)}, u32[]{:S(2)}) copy-start(s32[6]{0:T(128)} %copy-done.8) | copy-start | bytes 76
  423.5 17.4 %copy-start.1 = (f32[4,256,256]{2,1,0:T(8,128)S(1)}, f32[4,256,256]{2,1,0:T(8,128)}, u32[]{:S(2)}) copy-start(f32[4,256,256]{2,1,0:T(8,128)} %copy-done) | copy-start | bytes 3145732
  423.5 17.4 %copy-start.3 = (f32[6144]{0:T(1024)S(1)}, f32[6144]{0:T(1024)}, u32[]{:S(2)}) copy-start(f32[6144]{0:T(1024)} %param.6) | copy-start | bytes 73732
  423.5 17.4 %copy-start.5 = (s32[10,8]{1,0:T(8,128)S(1)}, s32[10,8]{1,0:T(8,128)}, u32[]{:S(2)}) copy-start(s32[10,8]{1,0:T(8,128)} %copy-done.4) | copy-start | bytes 964
Sparse Core Ops, SparseCore 0:
  56.0 48.4 all-gather.6
  108.1 51.4 all-gather.8
  167.2 82.0 all-gather.10
